TPU v7x, 32 devices: a whole 2x2x4 slice. The times are simulated.
32 devices in a mesh: dp: 8 (over z, x), fsdp: 4 (over y, core).
Axes of the slice: x: 2, y: 2, z: 4, core: 2. Of those that a mesh axis runs over, the one named last changes fastest.
Arguments:
- dec_input: bfloat16 [32, 1024, 512], P('dp', 'fsdp'), may hold values from -6 to 6
- enc_output: bfloat16 [32, 1024, 512], P('dp', 'fsdp'), may hold values from -6 to 6
- dec_lengths: int32 [32], P('dp'), may hold values from 256 to 1024, as said below
- enc_lengths: int32 [32], P('dp'), may hold values from 256 to 1024, as said below
- lang_tags: int32 [32], P('dp'), may hold values from 0 to 15
- lang_table: bfloat16 [512, 16], P(('dp', 'fsdp')), may hold values from -3 to 3
- self_in: bfloat16 [512, 1536], P(('dp', 'fsdp')), may hold values from -0.25 to 0.25
- self_out: bfloat16 [512, 512], P(('dp', 'fsdp')), may hold values from -2 to 2
- cross_q: bfloat16 [512, 512], P(('dp', 'fsdp')), may hold values from -0.25 to 0.25
- cross_kv: bfloat16 [512, 1024], P(('dp', 'fsdp')), may hold values from -0.25 to 0.25
- cross_out: bfloat16 [512, 512], P(('dp', 'fsdp')), may hold values from -2 to 2
- ffn_in: bfloat16 [512, 2048], P(('dp', 'fsdp')), may hold values from -0.25 to 0.25
- ffn_out: bfloat16 [2048, 512], P(('dp', 'fsdp')), may hold values from -0.125 to 0.125
- biases: bfloat16 [512, 7], P(('dp', 'fsdp')), may hold values from -2 to 2
- ffn_bias: bfloat16 [2048], P(('dp', 'fsdp')), may hold values from -2 to 2
- norm_gains: bfloat16 [512, 3], P(('dp', 'fsdp')), may hold values from 0.5 to 1.5
- norm_shifts: bfloat16 [512, 3], P(('dp', 'fsdp')), may hold values from -2 to 2
- cotangent: float32 [32, 1024, 512], P('dp', 'fsdp'), may hold values from -6 to 6
Outputs:
- output: bfloat16 [32, 1024, 512], P('dp', 'fsdp')
- grad_input: float32 [32, 1024, 512], P('dp', 'fsdp')
- grad_encoder: float32 [32, 1024, 512], P('dp', 'fsdp')
- grad_lang_table: float32 [512, 16], P(('dp', 'fsdp'))
- grad_self_in: float32 [512, 1536], P(('dp', 'fsdp'))
- grad_self_out: float32 [512, 512], P(('dp', 'fsdp'))
- grad_cross_q: float32 [512, 512], P(('dp', 'fsdp'))
- grad_cross_kv: float32 [512, 1024], P(('dp', 'fsdp'))
- grad_cross_out: float32 [512, 512], P(('dp', 'fsdp'))
- grad_ffn_in: float32 [512, 2048], P(('dp', 'fsdp'))
- grad_ffn_out: float32 [2048, 512], P(('dp', 'fsdp'))
- grad_biases: float32 [512, 7], P(('dp', 'fsdp'))
- grad_ffn_bias: float32 [2048], P(('dp', 'fsdp'))
- grad_norm_gains: float32 [512, 3], P(('dp', 'fsdp'))
- grad_norm_shifts: float32 [512, 3], P(('dp', 'fsdp'))
Inputs may be any that keep to these rules, and one draw needn't show every extreme that they name: `dec_lengths`: in each aligned block of 4 sequences one has length 1024. `enc_lengths`: in each aligned block of 4 sequences one has length 1024.
All inputs are finite; a program needn't handle non-finite values.
Results may differ from a plain program's by a relative error of at most 0.022.
The roundings to bfloat16 on the way count: a program that leaves them out, or rounds other values in their place, can miss the bound.
Values may be sent and summed in bfloat16 or wider, within the bound.
A program may use at most 320 MiB of HBM per device.

v0:
```python
import math

import jax
import jax.numpy as jnp
from jax import lax
from jax.sharding import PartitionSpec as P

HEADS = 8


def smooth_gelu(values):
    return (
        0.5
        * values
        * (1.0 + jnp.tanh(0.7978845608028654 * (values + 0.044715 * values * values * values)))
    )


def times_t(left, right):
    return lax.dot_general(
        left, right, (((1,), (1,)), ((), ())), preferred_element_type=jnp.float32
    )


def outer_sum(left, right):
    return lax.dot_general(
        left, right, (((0,), (0,)), ((), ())), preferred_element_type=jnp.float32
    )


def normalize_rows(residual, gain_col, shift_col):
    row_mean = jnp.mean(residual, axis=-1, keepdims=True)
    centered = residual - row_mean
    inv_dev = lax.rsqrt(jnp.mean(centered * centered, axis=-1, keepdims=True) + 1e-05)
    unit_rows = centered * inv_dev
    return (unit_rows * gain_col + shift_col, unit_rows, inv_dev)


def normalize_back(grad_above, unit_rows, inv_dev, gain_col):
    grad_unit = grad_above * gain_col
    grad_res = inv_dev * (
        grad_unit
        - jnp.mean(grad_unit, axis=-1, keepdims=True)
        - unit_rows * jnp.mean(grad_unit * unit_rows, axis=-1, keepdims=True)
    )
    return (grad_res, jnp.sum(grad_above * unit_rows, axis=0), jnp.sum(grad_above, axis=0))


def masked_scores(query_bf, key_full, lengths_here):
    groups, rows_here, features = query_bf.shape
    key_count = key_full.shape[1]
    head_size = features // HEADS
    query_heads = query_bf.reshape(groups, rows_here, HEADS, head_size)
    key_heads = key_full.reshape(groups, key_count, HEADS, head_size)
    scores = jnp.einsum(
        "sqhd,skhd->shqk", query_heads, key_heads, preferred_element_type=jnp.float32
    ) * (1.0 / math.sqrt(head_size))
    key_valid = jnp.arange(key_count)[None, :] < lengths_here[:, None]
    return jnp.where(key_valid[:, None, None, :], scores, -1000000000.0)


def attend_forward(query_bf, key_full, value_full, lengths_here):
    groups, rows_here, features = query_bf.shape
    key_count = key_full.shape[1]
    value_heads = value_full.reshape(groups, key_count, HEADS, features // HEADS)
    scores = masked_scores(query_bf, key_full, lengths_here)
    row_max = jnp.max(scores, axis=-1, keepdims=True)
    exp_scores = jnp.exp(scores - row_max)
    row_total = jnp.sum(exp_scores, axis=-1, keepdims=True)
    probs_bf = (exp_scores / row_total).astype(jnp.bfloat16)
    attn_mixed = jnp.einsum(
        "shqk,skhd->sqhd", probs_bf, value_heads, preferred_element_type=jnp.float32
    )
    return (attn_mixed.reshape(groups, rows_here, features), row_max + jnp.log(row_total))


def attend_back(grad_mixed_bf, query_bf, key_full, value_full, lengths_here, log_total):
    groups, rows_here, features = query_bf.shape
    key_count = key_full.shape[1]
    head_size = features // HEADS
    query_heads = query_bf.reshape(groups, rows_here, HEADS, head_size)
    key_heads = key_full.reshape(groups, key_count, HEADS, head_size)
    value_heads = value_full.reshape(groups, key_count, HEADS, head_size)
    grad_heads = grad_mixed_bf.reshape(groups, rows_here, HEADS, head_size)
    attn_probs = jnp.exp(masked_scores(query_bf, key_full, lengths_here) - log_total)
    probs_bf = attn_probs.astype(jnp.bfloat16)
    grad_probs = jnp.einsum(
        "sqhd,skhd->shqk", grad_heads, value_heads, preferred_element_type=jnp.float32
    )
    grad_values = jnp.einsum(
        "shqk,sqhd->skhd", probs_bf, grad_heads, preferred_element_type=jnp.float32
    )
    grad_scores = attn_probs * (
        grad_probs - jnp.sum(attn_probs * grad_probs, axis=-1, keepdims=True)
    )
    grad_scores_bf = grad_scores.astype(jnp.bfloat16)
    score_scale = 1.0 / math.sqrt(head_size)
    grad_query = (
        jnp.einsum("shqk,skhd->sqhd", grad_scores_bf, key_heads, preferred_element_type=jnp.float32)
        * score_scale
    )
    grad_keys = (
        jnp.einsum(
            "shqk,sqhd->skhd", grad_scores_bf, query_heads, preferred_element_type=jnp.float32
        )
        * score_scale
    )
    return (
        grad_query.reshape(groups, rows_here, features),
        grad_keys.reshape(groups, key_count, features),
        grad_values.reshape(groups, key_count, features),
    )


def body(
    dec_input,
    enc_output,
    dec_lengths,
    enc_lengths,
    lang_tags,
    lang_table,
    self_in,
    self_out,
    cross_q,
    cross_kv,
    cross_out,
    ffn_in,
    ffn_out,
    biases,
    ffn_bias,
    norm_gains,
    norm_shifts,
    cotangent,
):
    full_weights = (
        lax.all_gather(lang_table, ("dp", "fsdp"), axis=0, tiled=True),
        lax.all_gather(self_in, ("dp", "fsdp"), axis=0, tiled=True),
        lax.all_gather(self_out, ("dp", "fsdp"), axis=0, tiled=True),
        lax.all_gather(cross_q, ("dp", "fsdp"), axis=0, tiled=True),
        lax.all_gather(cross_kv, ("dp", "fsdp"), axis=0, tiled=True),
        lax.all_gather(cross_out, ("dp", "fsdp"), axis=0, tiled=True),
        lax.all_gather(ffn_in, ("dp", "fsdp"), axis=0, tiled=True),
        lax.all_gather(ffn_out, ("dp", "fsdp"), axis=0, tiled=True),
        lax.all_gather(biases, ("dp", "fsdp"), axis=0, tiled=True),
        lax.all_gather(ffn_bias, ("dp", "fsdp"), axis=0, tiled=True),
        lax.all_gather(norm_gains, ("dp", "fsdp"), axis=0, tiled=True),
        lax.all_gather(norm_shifts, ("dp", "fsdp"), axis=0, tiled=True),
    )
    (
        full_table,
        full_in,
        full_out,
        full_cq,
        full_ckv,
        full_co,
        full_ffn_in,
        full_ffn_out,
        full_biases,
        full_ffn_bias,
        full_gains,
        full_shifts,
    ) = full_weights
    bias_cols = full_biases.astype(jnp.float32)
    gain_cols = full_gains.astype(jnp.float32)
    shift_cols = full_shifts.astype(jnp.float32)
    groups, rows_here, features = dec_input.shape
    enc_rows = enc_output.shape[1]
    tokens = groups * rows_here
    positions = lax.axis_index("fsdp") * rows_here + jnp.arange(rows_here)
    live_rows = (positions[None, :] < dec_lengths[:, None]).astype(jnp.float32)
    live_flat = live_rows.reshape(tokens, 1)
    onehot = (lang_tags[:, None] == jnp.arange(full_table.shape[1])[None, :]).astype(jnp.float32)
    lang_rows = lax.dot_general(
        onehot,
        full_table.astype(jnp.float32),
        (((1,), (1,)), ((), ())),
        precision=lax.Precision.HIGHEST,
        preferred_element_type=jnp.float32,
    )
    flat_start = (dec_input.astype(jnp.float32) + lang_rows[:, None, :]).reshape(tokens, features)
    start_bf = flat_start.astype(jnp.bfloat16)
    zeros_row = jnp.zeros((features,), jnp.float32)
    merged = (
        jnp.dot(start_bf, full_in, preferred_element_type=jnp.float32)
        + jnp.concatenate([bias_cols[:, 0], zeros_row, bias_cols[:, 1]])[None, :]
    )
    merged_bf = merged.astype(jnp.bfloat16).reshape(groups, rows_here, 3 * features)
    query_bf = merged_bf[:, :, :features]
    key_own = merged_bf[:, :, features : 2 * features]
    value_own = merged_bf[:, :, 2 * features :]
    key_full, value_full = (
        lax.all_gather(key_own, "fsdp", axis=1, tiled=True),
        lax.all_gather(value_own, "fsdp", axis=1, tiled=True),
    )
    attn_mixed, self_lse = attend_forward(query_bf, key_full, value_full, dec_lengths)
    mixed_bf = attn_mixed.astype(jnp.bfloat16).reshape(tokens, features)
    branch = jnp.dot(mixed_bf, full_out, preferred_element_type=jnp.float32) + bias_cols[:, 2]
    normed_one, unit_one, inv_one = normalize_rows(
        flat_start + branch, gain_cols[:, 0], shift_cols[:, 0]
    )
    one_bf = normed_one.astype(jnp.bfloat16)
    cross_query = (
        (jnp.dot(one_bf, full_cq, preferred_element_type=jnp.float32) + bias_cols[:, 3])
        .astype(jnp.bfloat16)
        .reshape(groups, rows_here, features)
    )
    enc_flat = enc_output.reshape(groups * enc_rows, features)
    cross_pair = (
        jnp.dot(enc_flat, full_ckv, preferred_element_type=jnp.float32)
        + jnp.concatenate([zeros_row, bias_cols[:, 4]])[None, :]
    )
    pair_bf = cross_pair.astype(jnp.bfloat16).reshape(groups, enc_rows, 2 * features)
    ckey_own = pair_bf[:, :, :features]
    cvalue_own = pair_bf[:, :, features:]
    ckey_full, cvalue_full = (
        lax.all_gather(ckey_own, "fsdp", axis=1, tiled=True),
        lax.all_gather(cvalue_own, "fsdp", axis=1, tiled=True),
    )
    cross_mixed, cross_lse = attend_forward(cross_query, ckey_full, cvalue_full, enc_lengths)
    cmixed_bf = cross_mixed.astype(jnp.bfloat16).reshape(tokens, features)
    cross_branch = jnp.dot(cmixed_bf, full_co, preferred_element_type=jnp.float32) + bias_cols[:, 5]
    normed_two, unit_two, inv_two = normalize_rows(
        normed_one + cross_branch, gain_cols[:, 1], shift_cols[:, 1]
    )
    two_bf = normed_two.astype(jnp.bfloat16)
    hidden = jnp.dot(
        two_bf, full_ffn_in, preferred_element_type=jnp.float32
    ) + full_ffn_bias.astype(jnp.float32)
    activated, gelu_pull = jax.vjp(smooth_gelu, hidden)
    act_bf = activated.astype(jnp.bfloat16)
    ffn_branch = jnp.dot(act_bf, full_ffn_out, preferred_element_type=jnp.float32) + bias_cols[:, 6]
    normed_three, unit_three, inv_three = normalize_rows(
        normed_two + ffn_branch, gain_cols[:, 2], shift_cols[:, 2]
    )
    output = (normed_three * live_flat).astype(jnp.bfloat16).reshape(groups, rows_here, features)
    back_weights = (
        lax.all_gather(lang_table, ("dp", "fsdp"), axis=0, tiled=True),
        lax.all_gather(self_in, ("dp", "fsdp"), axis=0, tiled=True),
        lax.all_gather(self_out, ("dp", "fsdp"), axis=0, tiled=True),
        lax.all_gather(cross_q, ("dp", "fsdp"), axis=0, tiled=True),
        lax.all_gather(cross_kv, ("dp", "fsdp"), axis=0, tiled=True),
        lax.all_gather(cross_out, ("dp", "fsdp"), axis=0, tiled=True),
        lax.all_gather(ffn_in, ("dp", "fsdp"), axis=0, tiled=True),
        lax.all_gather(ffn_out, ("dp", "fsdp"), axis=0, tiled=True),
        lax.all_gather(biases, ("dp", "fsdp"), axis=0, tiled=True),
        lax.all_gather(ffn_bias, ("dp", "fsdp"), axis=0, tiled=True),
        lax.all_gather(norm_gains, ("dp", "fsdp"), axis=0, tiled=True),
        lax.all_gather(norm_shifts, ("dp", "fsdp"), axis=0, tiled=True),
    )
    back_in = back_weights[1]
    back_out = back_weights[2]
    back_cq = back_weights[3]
    back_ckv = back_weights[4]
    back_co = back_weights[5]
    back_ffn_in = back_weights[6]
    back_ffn_out = back_weights[7]
    back_gains = back_weights[10].astype(jnp.float32)
    grad_above = cotangent.reshape(tokens, features) * live_flat
    grad_res3, gain_three, shift_three = normalize_back(
        grad_above, unit_three, inv_three, back_gains[:, 2]
    )
    grad_low3 = grad_res3.astype(jnp.bfloat16)
    grad_ffn_out = outer_sum(act_bf, grad_low3)
    bias_six = jnp.sum(grad_low3.astype(jnp.float32), axis=0)
    grad_act = times_t(grad_low3, back_ffn_out)
    grad_hidden_bf = gelu_pull(grad_act)[0].astype(jnp.bfloat16)
    grad_ffn_in = outer_sum(two_bf, grad_hidden_bf)
    grad_ffn_bias = jnp.sum(grad_hidden_bf.astype(jnp.float32), axis=0)
    grad_two = grad_res3 + times_t(grad_hidden_bf, back_ffn_in)
    grad_res2, gain_two, shift_two = normalize_back(grad_two, unit_two, inv_two, back_gains[:, 1])
    grad_low2 = grad_res2.astype(jnp.bfloat16)
    grad_cross_out = outer_sum(cmixed_bf, grad_low2)
    bias_five = jnp.sum(grad_low2.astype(jnp.float32), axis=0)
    grad_cmixed = (
        times_t(grad_low2, back_co).astype(jnp.bfloat16).reshape(groups, rows_here, features)
    )
    grad_cquery, grad_ckey, grad_cvalue = attend_back(
        grad_cmixed, cross_query, ckey_full, cvalue_full, enc_lengths, cross_lse
    )
    ckey_sum, cvalue_sum = (
        lax.psum_scatter(
            grad_ckey.astype(jnp.bfloat16), "fsdp", scatter_dimension=1, tiled=True
        ).astype(jnp.float32),
        lax.psum_scatter(
            grad_cvalue.astype(jnp.bfloat16), "fsdp", scatter_dimension=1, tiled=True
        ).astype(jnp.float32),
    )
    grad_pair_bf = (
        jnp.concatenate([ckey_sum, cvalue_sum], axis=-1)
        .astype(jnp.bfloat16)
        .reshape(groups * enc_rows, 2 * features)
    )
    grad_cross_kv = outer_sum(enc_flat, grad_pair_bf)
    bias_four = jnp.sum(grad_pair_bf[:, features:].astype(jnp.float32), axis=0)
    grad_encoder = times_t(grad_pair_bf, back_ckv).reshape(groups, enc_rows, features)
    grad_cquery_bf = grad_cquery.astype(jnp.bfloat16).reshape(tokens, features)
    grad_cross_q = outer_sum(one_bf, grad_cquery_bf)
    bias_three = jnp.sum(grad_cquery_bf.astype(jnp.float32), axis=0)
    grad_one = grad_res2 + times_t(grad_cquery_bf, back_cq)
    grad_res1, gain_one, shift_one = normalize_back(grad_one, unit_one, inv_one, back_gains[:, 0])
    grad_low1 = grad_res1.astype(jnp.bfloat16)
    grad_self_out = outer_sum(mixed_bf, grad_low1)
    bias_two = jnp.sum(grad_low1.astype(jnp.float32), axis=0)
    grad_mixed = (
        times_t(grad_low1, back_out).astype(jnp.bfloat16).reshape(groups, rows_here, features)
    )
    grad_query, grad_key, grad_value = attend_back(
        grad_mixed, query_bf, key_full, value_full, dec_lengths, self_lse
    )
    key_sum, value_sum = (
        lax.psum_scatter(
            grad_key.astype(jnp.bfloat16), "fsdp", scatter_dimension=1, tiled=True
        ).astype(jnp.float32),
        lax.psum_scatter(
            grad_value.astype(jnp.bfloat16), "fsdp", scatter_dimension=1, tiled=True
        ).astype(jnp.float32),
    )
    grad_merged_bf = (
        jnp.concatenate([grad_query, key_sum, value_sum], axis=-1)
        .astype(jnp.bfloat16)
        .reshape(tokens, 3 * features)
    )
    grad_self_in = outer_sum(start_bf, grad_merged_bf)
    merged_sums = jnp.sum(grad_merged_bf.astype(jnp.float32), axis=0)
    grad_start = grad_res1 + times_t(grad_merged_bf, back_in)
    grad_input = grad_start.reshape(groups, rows_here, features)
    seq_sums = jnp.sum(grad_input, axis=1)
    grad_table = lax.dot_general(
        seq_sums,
        onehot,
        (((0,), (0,)), ((), ())),
        precision=lax.Precision.HIGHEST,
        preferred_element_type=jnp.float32,
    )
    grad_biases = jnp.stack(
        [
            merged_sums[:features],
            merged_sums[2 * features :],
            bias_two,
            bias_three,
            bias_four,
            bias_five,
            bias_six,
        ],
        axis=1,
    )
    grad_gains = jnp.stack([gain_one, gain_two, gain_three], axis=1)
    grad_shifts = jnp.stack([shift_one, shift_two, shift_three], axis=1)
    reduced = (
        lax.psum_scatter(grad_table, ("dp", "fsdp"), scatter_dimension=0, tiled=True),
        lax.psum_scatter(grad_self_in, ("dp", "fsdp"), scatter_dimension=0, tiled=True),
        lax.psum_scatter(grad_self_out, ("dp", "fsdp"), scatter_dimension=0, tiled=True),
        lax.psum_scatter(grad_cross_q, ("dp", "fsdp"), scatter_dimension=0, tiled=True),
        lax.psum_scatter(grad_cross_kv, ("dp", "fsdp"), scatter_dimension=0, tiled=True),
        lax.psum_scatter(grad_cross_out, ("dp", "fsdp"), scatter_dimension=0, tiled=True),
        lax.psum_scatter(grad_ffn_in, ("dp", "fsdp"), scatter_dimension=0, tiled=True),
        lax.psum_scatter(grad_ffn_out, ("dp", "fsdp"), scatter_dimension=0, tiled=True),
        lax.psum_scatter(grad_biases, ("dp", "fsdp"), scatter_dimension=0, tiled=True),
        lax.psum_scatter(grad_ffn_bias, ("dp", "fsdp"), scatter_dimension=0, tiled=True),
        lax.psum_scatter(grad_gains, ("dp", "fsdp"), scatter_dimension=0, tiled=True),
        lax.psum_scatter(grad_shifts, ("dp", "fsdp"), scatter_dimension=0, tiled=True),
    )
    return (
        output,
        grad_input,
        grad_encoder,
        reduced[0],
        reduced[1],
        reduced[2],
        reduced[3],
        reduced[4],
        reduced[5],
        reduced[6],
        reduced[7],
        reduced[8],
        reduced[9],
        reduced[10],
        reduced[11],
    )


def solution(mesh):
    return jax.shard_map(
        body,
        mesh=mesh,
        in_specs=(
            P("dp", "fsdp", None),
            P("dp", "fsdp", None),
            P("dp"),
            P("dp"),
            P("dp"),
            P(("dp", "fsdp"), None),
            P(("dp", "fsdp"), None),
            P(("dp", "fsdp"), None),
            P(("dp", "fsdp"), None),
            P(("dp", "fsdp"), None),
            P(("dp", "fsdp"), None),
            P(("dp", "fsdp"), None),
            P(("dp", "fsdp"), None),
            P(("dp", "fsdp"), None),
            P(("dp", "fsdp")),
            P(("dp", "fsdp"), None),
            P(("dp", "fsdp"), None),
            P("dp", "fsdp", None),
        ),
        out_specs=(
            P("dp", "fsdp", None),
            P("dp", "fsdp", None),
            P("dp", "fsdp", None),
            P(("dp", "fsdp"), None),
            P(("dp", "fsdp"), None),
            P(("dp", "fsdp"), None),
            P(("dp", "fsdp"), None),
            P(("dp", "fsdp"), None),
            P(("dp", "fsdp"), None),
            P(("dp", "fsdp"), None),
            P(("dp", "fsdp"), None),
            P(("dp", "fsdp"), None),
            P(("dp", "fsdp")),
            P(("dp", "fsdp"), None),
            P(("dp", "fsdp"), None),
        ),
        check_vma=False,
    )
```

profile of v0, /device:TPU:0, one launch (start us, length us, event | category | flops | bytes accessed | tf_op | source)
XLA Modules:
  0.0 2322.8 jit_solution(12795212375830996637)
XLA Ops:
  8.7 43.6 %all-gather = bf16[32,16,7]{1,2,0:T(8,128)(2,1)S(1)} all-gather(bf16[1,16,7]{1,2,0:T(8,128)(2,1)} %bitcast.241), channel_id=1, replica_groups=mesh['dp'=8,'fsdp'=4] {'dp','fsdp'}, dimensions={0}, use_global_device_ids=true | all-gather | bytes 7392 | tf_op jit(solution)/shard_map/all_gather | solution.py:144
  72.0 40.1 %all_gather.56 = bf16[512,16]{1,0:T(8,128)(2,1)S(1)} all-gather(bf16[16,16]{1,0:T(8,128)(2,1)S(1)} %copy-done.64), channel_id=1, replica_groups=mesh['dp'=8,'fsdp'=4] {'dp','fsdp'}, dimensions={0}, use_global_device_ids=true | all-gather | bytes 16896 | tf_op jit(solution)/shard_map/all_gather | solution.py:136
  131.9 39.1 %all-reduce.1 = bf16[2048]{0:T(1024)(128)(2,1)S(1)} all-reduce(bf16[2048]{0:T(1024)(128)(2,1)S(1)} %dynamic-update-slice), channel_id=1, replica_groups=mesh['dp'=8,'fsdp'=4] {'dp','fsdp'}, use_global_device_ids=true, to_apply=%add.1 | all-reduce | flops 2048 | bytes 8192
  172.3 40.0 %all-gather.1 = bf16[32,16,3]{1,2,0:T(4,128)(2,1)S(1)} all-gather(bf16[1,16,3]{1,2,0:T(4,128)(2,1)S(1)} %bitcast.244), channel_id=1, replica_groups=mesh['dp'=8,'fsdp'=4] {'dp','fsdp'}, dimensions={0}, use_global_device_ids=true | all-gather | bytes 3168 | tf_op jit(solution)/shard_map/all_gather | solution.py:146
  212.4 36.7 %all-gather.2 = bf16[32,16,3]{1,2,0:T(4,128)(2,1)S(1)} all-gather(bf16[1,16,3]{1,2,0:T(4,128)(2,1)S(1)} %bitcast.245), channel_id=1, replica_groups=mesh['dp'=8,'fsdp'=4] {'dp','fsdp'}, dimensions={0}, use_global_device_ids=true | all-gather | bytes 3168 | tf_op jit(solution)/shard_map/all_gather | solution.py:147
  252.3 42.6 %all_gather.61 = bf16[512,512]{1,0:T(8,128)(2,1)} all-gather(bf16[16,512]{1,0:T(8,128)(2,1)S(1)} %copy-done.53), channel_id=1, replica_groups=mesh['dp'=8,'fsdp'=4] {'dp','fsdp'}, dimensions={0}, use_global_device_ids=true | all-gather | bytes 540672 | tf_op jit(solution)/shard_map/all_gather | solution.py:138
  294.9 41.2 %all_gather.66 = bf16[512,512]{1,0:T(8,128)(2,1)} all-gather(bf16[16,512]{1,0:T(8,128)(2,1)S(1)} %copy-done.54), channel_id=1, replica_groups=mesh['dp'=8,'fsdp'=4] {'dp','fsdp'}, dimensions={0}, use_global_device_ids=true | all-gather | bytes 540672 | tf_op jit(solution)/shard_map/all_gather | solution.py:139
  336.1 42.8 %all_gather.68 = bf16[512,512]{1,0:T(8,128)(2,1)} all-gather(bf16[16,512]{1,0:T(8,128)(2,1)S(1)} %copy-done.55), channel_id=1, replica_groups=mesh['dp'=8,'fsdp'=4] {'dp','fsdp'}, dimensions={0}, use_global_device_ids=true | all-gather | bytes 540672 | tf_op jit(solution)/shard_map/all_gather | solution.py:141
  558.2 26.1 %multiply_reduce_fusion.1 = (f32[4,8,256]{2,1,0:T(8,128)S(1)}, f32[4,8,256,1024]{3,2,1,0:T(8,128)}) fusion(f32[4,8,256]{2,1,0:T(8,128)S(1)} %log_add_fusion.1, f32[4,8,256,1024]{3,2,1,0:T(8,128)} %get-tuple-element.121, pred[4,1024]{1,0:T(4,128)(4,1)S(1)} %iota_compare_fusion, bf16[4,256,8,64]{1,3,2,0:T(8,128)(2,1)} %copy.122, ...), kind=kOutput, calls=%fused_computation.4 | convolution fusion | flops 1115676672 | bytes 72421376 | tf_op jit(solution)/shard_map/sqhd,skhd->shqk/dot_general | solution.py:87
  584.3 27.8 %multiply_convert_fusion.1 = bf16[4,8,256,1024]{3,2,1,0:T(8,128)(2,1)} fusion(f32[4,8,256,1024]{3,2,1,0:T(8,128)} %get-tuple-element.128, f32[4,8,256]{2,1,0:T(8,128)S(1)} %get-tuple-element.127, f32[4,8,256]{2,1,0:T(8,128)S(1)} %log_add_fusion.1, f32[4,8,256,1024]{3,2,1,0:T(8,128)} %get-tuple-element.121, pred[4,1024]{1,0:T(4,128)(4,1)S(1)} %iota_compare_fusion), kind=kLoop, calls=%fused_computation.3 | loop fusion | flops 50331648 | bytes 83955712 | tf_op jit(solution)/shard_map/convert_element_type | solution.py:96
  658.6 27.2 %multiply_reduce_fusion = (f32[4,8,256]{2,1,0:T(8,128)S(1)}, f32[4,8,256,1024]{3,2,1,0:T(8,128)}) fusion(f32[4,8,256]{2,1,0:T(8,128)S(1)} %log_add_fusion, f32[4,8,256,1024]{3,2,1,0:T(8,128)} %get-tuple-element.117, pred[4,1024]{1,0:T(4,128)(4,1)S(1)} %copy-done.40, bf16[4,256,8,64]{1,3,2,0:T(8,128)(2,1)S(1)} %copy-done.23, ...), kind=kOutput, calls=%fused_computation.1 | convolution fusion | flops 1115676672 | bytes 72421376 | tf_op jit(solution)/shard_map/sqhd,skhd->shqk/dot_general | solution.py:87
  685.8 28.2 %multiply_convert_fusion = bf16[4,8,256,1024]{3,2,1,0:T(8,128)(2,1)} fusion(f32[4,8,256,1024]{3,2,1,0:T(8,128)} %get-tuple-element.131, f32[4,8,256]{2,1,0:T(8,128)S(1)} %get-tuple-element.130, f32[4,8,256]{2,1,0:T(8,128)S(1)} %log_add_fusion, f32[4,8,256,1024]{3,2,1,0:T(8,128)} %get-tuple-element.117, pred[4,1024]{1,0:T(4,128)(4,1)S(1)} %copy-done.40), kind=kLoop, calls=%fused_computation | loop fusion | flops 50331648 | bytes 83955712 | tf_op jit(solution)/shard_map/convert_element_type | solution.py:96
  879.6 39.5 %all-reduce.2 = f32[2048]{0:T(1024)S(1)} all-reduce(f32[2048]{0:T(1024)S(1)} %copy-done.62), channel_id=15, replica_groups=mesh['dp'=8,'fsdp'=4] {'dp','fsdp'}, use_global_device_ids=true, to_apply=%region_39.40.clone | all-reduce | flops 2048 | bytes 16384
  919.7 82.0 %reduce-scatter.52.cloned.1.call-done = f32[16,3]{1,0:T(8,128)} async-done(((f32[512,3]{1,0:T(8,128)}), f32[16,3]{1,0:T(8,128)}) %reduce-scatter.52.cloned.1.call-update) | async-done | bytes 208
  1003.1 130.2 %reduce-scatter.50.cloned.1.call-done = f32[16,3]{1,0:T(8,128)} async-done(((f32[512,3]{1,0:T(8,128)}), f32[16,3]{1,0:T(8,128)}) %reduce-scatter.50.cloned.1.call-update) | async-done | bytes 208
  1139.1 125.6 %reduce-scatter.48.cloned.1.call-done = f32[16,7]{1,0:T(8,128)} async-done(((f32[512,7]{1,0:T(8,128)}), f32[16,7]{1,0:T(8,128)}) %reduce-scatter.48.cloned.1.call-update) | async-done | bytes 464
  1266.1 132.1 %reduce-scatter.40.cloned.1.call-done = f32[16,512]{1,0:T(8,128)} async-done(((f32[512,512]{1,0:T(8,128)}), f32[16,512]{1,0:T(8,128)}) %reduce-scatter.40.cloned.1.call-update) | async-done | bytes 32784 | tf_op jit(solution)/shard_map/reduce_scatter | solution.py:355
  1398.2 133.4 %reduce-scatter.38.cloned.1.call-done = f32[16,512]{1,0:T(8,128)} async-done(((f32[512,512]{1,0:T(8,128)}), f32[16,512]{1,0:T(8,128)}) %reduce-scatter.38.cloned.1.call-update) | async-done | bytes 32784 | tf_op jit(solution)/shard_map/reduce_scatter | solution.py:353
  1531.5 133.5 %reduce-scatter.36.cloned.1.call-done = f32[16,512]{1,0:T(8,128)} async-done(((f32[512,512]{1,0:T(8,128)}), f32[16,512]{1,0:T(8,128)}) %reduce-scatter.36.cloned.1.call-update) | async-done | bytes 32784 | tf_op jit(solution)/shard_map/reduce_scatter | solution.py:352
  1665.0 139.9 %reduce-scatter.44.cloned.1.call-done = f32[64,512]{1,0:T(8,128)} async-done(((f32[2048,512]{1,0:T(8,128)}), f32[64,512]{1,0:T(8,128)}) %reduce-scatter.44.cloned.1.call-update) | async-done | bytes 131088 | tf_op jit(solution)/shard_map/reduce_scatter | solution.py:357
  1804.9 139.7 %reduce-scatter.42.cloned.1.call-done = f32[16,2048]{1,0:T(8,128)} async-done(((f32[512,2048]{1,0:T(8,128)}), f32[16,2048]{1,0:T(8,128)}) %reduce-scatter.42.cloned.1.call-update) | async-done | bytes 131088 | tf_op jit(solution)/shard_map/reduce_scatter | solution.py:356
  1944.6 132.1 %reduce-scatter.32.cloned.1.call-done = f32[16,16]{1,0:T(8,128)} async-done(((f32[512,16]{1,0:T(8,128)}), f32[16,16]{1,0:T(8,128)}) %reduce-scatter.32.cloned.1.call-update) | async-done | bytes 1040 | tf_op jit(solution)/shard_map/reduce_scatter | solution.py:350
  2076.7 135.7 %reduce-scatter.46.cloned.1.call-done = f32[16,1024]{1,0:T(8,128)} async-done(((f32[512,1024]{1,0:T(8,128)}), f32[16,1024]{1,0:T(8,128)}) %reduce-scatter.46.cloned.1.call-update) | async-done | bytes 65552
  2212.4 103.5 %reduce-scatter.34.cloned.1.call-done = f32[16,1536]{1,0:T(8,128)} async-done(((f32[512,1536]{1,0:T(8,128)}), f32[16,1536]{1,0:T(8,128)}) %reduce-scatter.34.cloned.1.call-update) | async-done | bytes 98320 | tf_op jit(solution)/shard_map/reduce_scatter | solution.py:351
  (344 shorter events, 444.6 us)
Async XLA Ops:
  7.2 60.1 %all-gather.18.cloned.1.call-start = ((), (), s32[]{:S(2)}) async-start(), calls=%async_computation.18 | async-start | bytes 1081344 | tf_op jit(solution)/shard_map/all_gather | solution.py:140
  7.9 116.3 %all-gather.12.cloned.1.call-start = ((), (), s32[]{:S(2)}) async-start(), calls=%async_computation.15 | async-start | bytes 1622016 | tf_op jit(solution)/shard_map/all_gather | solution.py:137
  8.7 371.8 %all-gather.22.cloned.1.call-start = ((), (), s32[]{:S(2)}) async-start(), calls=%async_computation.20 | async-start | bytes 5242880 | tf_op jit(solution)/shard_map/all_gather | solution.py:216
  71.4 315.7 %all-gather.20.cloned.1.call-start = ((), (), s32[]{:S(2)}) async-start(), calls=%async_computation.19 | async-start | bytes 5242880 | tf_op jit(solution)/shard_map/all_gather | solution.py:217
  72.0 321.4 %all-gather.16.cloned.1.call-start = ((), (), s32[]{:S(2)}) async-start(), calls=%async_computation.17 | async-start | bytes 5242880 | tf_op jit(solution)/shard_map/all_gather | solution.py:192
  129.3 300.4 %all-gather.14.cloned.1.call-start = ((), (), s32[]{:S(2)}) async-start(), calls=%async_computation.16 | async-start | bytes 5242880 | tf_op jit(solution)/shard_map/all_gather | solution.py:193
  129.9 382.9 %all-gather.24.cloned.1.call-start = ((), (), s32[]{:S(2)}) async-start(), calls=%async_computation.21 | async-start | bytes 2162688 | tf_op jit(solution)/shard_map/all_gather | solution.py:142
  130.6 390.1 %all-gather.26.cloned.1.call-start = ((), (), s32[]{:S(2)}) async-start(), calls=%async_computation.22 | async-start | bytes 2162688 | tf_op jit(solution)/shard_map/all_gather | solution.py:143
  131.4 661.8 %reduce-scatter.26.cloned.1.call-start = ((), (), s32[]{:S(2)}) async-start(), calls=%async_computation.24 | async-start | bytes 5242880 | tf_op jit(solution)/shard_map/reduce_scatter | solution.py:314
  131.6 304.4 %copy-start.39 = (pred[4,1024]{1,0:T(4,128)(4,1)}, pred[4,1024]{1,0:T(4,128)(4,1)S(1)}, u32[]{:S(2)}) copy-start(pred[4,1024]{1,0:T(4,128)(4,1)S(1)} %iota_compare_fusion.1) | copy-start | bytes 12292
  657.4 138.5 %reduce-scatter.24.cloned.1.call-start = ((), (), s32[]{:S(2)}) async-start(), calls=%async_computation.23 | async-start | bytes 5242880 | tf_op jit(solution)/shard_map/reduce_scatter | solution.py:311
  731.1 87.7 %reduce-scatter.30.cloned.1.call-start = ((), (), s32[]{:S(2)}) async-start(), calls=%async_computation.26 | async-start | bytes 5242880 | tf_op jit(solution)/shard_map/reduce_scatter | solution.py:284
  756.1 109.8 %reduce-scatter.28.cloned.1.call-start = ((), (), s32[]{:S(2)}) async-start(), calls=%async_computation.25 | async-start | bytes 5242880 | tf_op jit(solution)/shard_map/reduce_scatter | solution.py:281
  774.4 227.3 %reduce-scatter.52.cloned.1.call-start = ((), (), s32[]{:S(2)}) async-start(), calls=%async_computation.37 | async-start | bytes 270336
  790.1 343.2 %reduce-scatter.50.cloned.1.call-start = ((), (), s32[]{:S(2)}) async-start(), calls=%async_computation.36 | async-start | bytes 270336
  793.1 471.6 %reduce-scatter.48.cloned.1.call-start = ((), (), s32[]{:S(2)}) async-start(), calls=%async_computation.35 | async-start | bytes 270336
  821.2 577.0 %reduce-scatter.40.cloned.1.call-start = ((), (), s32[]{:S(2)}) async-start(), calls=%async_computation.31 | async-start | bytes 1081344 | tf_op jit(solution)/shard_map/reduce_scatter | solution.py:355
  824.2 707.3 %reduce-scatter.38.cloned.1.call-start = ((), (), s32[]{:S(2)}) async-start(), calls=%async_computation.30 | async-start | bytes 1081344 | tf_op jit(solution)/shard_map/reduce_scatter | solution.py:353
  827.7 837.3 %reduce-scatter.36.cloned.1.call-start = ((), (), s32[]{:S(2)}) async-start(), calls=%async_computation.29 | async-start | bytes 1081344 | tf_op jit(solution)/shard_map/reduce_scatter | solution.py:352
  830.7 974.2 %reduce-scatter.44.cloned.1.call-start = ((), (), s32[]{:S(2)}) async-start(), calls=%async_computation.33 | async-start | bytes 4325376 | tf_op jit(solution)/shard_map/reduce_scatter | solution.py:357
  841.6 1103.0 %reduce-scatter.42.cloned.1.call-start = ((), (), s32[]{:S(2)}) async-start(), calls=%async_computation.32 | async-start | bytes 4325376 | tf_op jit(solution)/shard_map/reduce_scatter | solution.py:356
  849.9 1226.8 %reduce-scatter.32.cloned.1.call-start = ((), (), s32[]{:S(2)}) async-start(), calls=%async_computation.27 | async-start | bytes 270336 | tf_op jit(solution)/shard_map/reduce_scatter | solution.py:350
  858.3 1354.1 %reduce-scatter.46.cloned.1.call-start = ((), (), s32[]{:S(2)}) async-start(), calls=%async_computation.34 | async-start | bytes 2162688
  874.5 1441.4 %reduce-scatter.34.cloned.1.call-start = ((), (), s32[]{:S(2)}) async-start(), calls=%async_computation.28 | async-start | bytes 3244032 | tf_op jit(solution)/shard_map/reduce_scatter | solution.py:351
  (78 other events, 1476.7 us)
Sparse Core Ops, SparseCore 0:
  10.9 56.3 all-gather.17
  70.2 54.0 all-gather.11
  126.4 34.1 all-gather.21
  162.6 34.7 all-gather.19
  198.8 34.6 all-gather.15
  234.9 36.6 all-gather.13
  274.5 57.5 all-gather.23
  335.0 55.8 all-gather.25
  657.5 40.6 reduce-scatter.25
  731.2 40.5 reduce-scatter.23
  774.3 44.4 reduce-scatter.29
  821.4 44.5 reduce-scatter.27
  868.2 133.5 reduce-scatter.51
  1003.9 129.3 reduce-scatter.49
  1135.3 129.3 reduce-scatter.47
  1267.5 130.6 reduce-scatter.39
  1400.8 130.6 reduce-scatter.37
  1534.3 130.6 reduce-scatter.35
  1667.8 137.0 reduce-scatter.43
  1807.6 136.9 reduce-scatter.41
  1947.4 129.2 reduce-scatter.31
  2079.6 132.6 reduce-scatter.45
  2218.4 97.4 reduce-scatter.33
where the time goes:
time: 2330 us; the launch traced here: 2320 us
  waiting for transfers between devices  1440 us (62%)
  blocking collectives  366 us (16%)
  matrix products  281 us (12%)
  local copies, waits for them, and re-layouts  117 us (5%)
  other arithmetic  99.8 us (4%)
    unnamed x27, waiting for transfers between devices  478 us
    reduce_scatter x1, waiting for transfers between devices, body(): lax.psum_scatter(grad_ffn_out, ('dp', 'fsdp'), scatter_dimension=0, tiled...  140 us
    reduce_scatter x1, waiting for transfers between devices, body(): lax.psum_scatter(grad_ffn_in, ('dp', 'fsdp'), scatter_dimension=0, tiled=...  140 us
    reduce_scatter x1, waiting for transfers between devices, body(): lax.psum_scatter(grad_self_out, ('dp', 'fsdp'), scatter_dimension=0, tile...  133 us
    reduce_scatter x1, waiting for transfers between devices, body(): lax.psum_scatter(grad_cross_q, ('dp', 'fsdp'), scatter_dimension=0, tiled...  133 us
    reduce_scatter x1, waiting for transfers between devices, body(): lax.psum_scatter(grad_table, ('dp', 'fsdp'), scatter_dimension=0, tiled=T...  132 us
    reduce_scatter x1, waiting for transfers between devices, body(): lax.psum_scatter(grad_cross_out, ('dp', 'fsdp'), scatter_dimension=0, til...  132 us
    reduce_scatter x1, waiting for transfers between devices, body(): lax.psum_scatter(grad_self_in, ('dp', 'fsdp'), scatter_dimension=0, tiled...  103 us
  transfers between devices with their start and end apart: 23, of which 15 were waited for; matrix products, arithmetic and copies ran while one was open for 15% of the time, Pallas kernels for 0%

commit v1 on v0

--- a/solution.py
+++ b/solution.py
@@ -1,8 +1,11 @@
+import functools
 import math
 
 import jax
 import jax.numpy as jnp
 from jax import lax
+from jax.experimental import pallas as pl
+from jax.experimental.pallas import tpu as pltpu
 from jax.sharding import PartitionSpec as P
 
 HEADS = 8
@@ -379,9 +382,776 @@
     )
 
 
+F32 = jnp.float32
+BF16 = jnp.bfloat16
+
+
+def nt_dot(left, right):
+    return lax.dot_general(left, right, (((1,), (1,)), ((), ())), preferred_element_type=F32)
+
+
+def nn_dot(left, right):
+    return jnp.dot(left, right, preferred_element_type=F32)
+
+
+def split_three(value):
+    high = value.astype(BF16)
+    rest = value - high.astype(F32)
+    middle = rest.astype(BF16)
+    return high, middle, (rest - middle.astype(F32)).astype(BF16)
+
+
+def key_extra(tokens, length):
+    lane = lax.broadcasted_iota(jnp.int32, (tokens, 128), 1) % 64
+    row = lax.broadcasted_iota(jnp.int32, (tokens, 128), 0)
+    masked = jnp.where(row < length, 0.0, -1e30)
+    return jnp.where(lane == 3, masked, jnp.where(lane < 3, 1.0, 0.0)).astype(BF16)
+
+
+def row_extra(lane, head, terms, mask_lane):
+    base = head * 64
+    out = jnp.where(lane == base + 3, mask_lane, 0.0).astype(F32)
+    for place, term in enumerate(terms):
+        out = jnp.where(lane == base + place, term.astype(F32), out)
+    return out.astype(BF16)
+
+
+def attend_fwd_core(block, length, q_ref, k_ref, v_ref, o_ref, of_ref, lse_ref, kx_ref, va_ref, vb_ref):
+    tokens = q_ref.shape[0]
+    kx_ref[:, :128] = k_ref[...]
+    kx_ref[:, 128:] = key_extra(tokens, length)
+    lane_full = lax.broadcasted_iota(jnp.int32, (tokens, 128), 1)
+    values = v_ref[...].astype(F32)
+    va_ref[...] = jnp.where(lane_full < 64, values, 1.0).astype(BF16)
+    vb_ref[...] = jnp.where(lane_full < 64, 1.0, values).astype(BF16)
+
+    def step(index, carry):
+        rows = pl.ds(pl.multiple_of(index * block, block), block)
+        lane = lax.broadcasted_iota(jnp.int32, (block, 128), 1)
+        query = q_ref[rows, :].astype(F32) * 0.125
+        halves, tops = [], []
+        for head, vx_ref in enumerate((va_ref, vb_ref)):
+            inside = (lane < 64) if head == 0 else (lane >= 64)
+            own = jnp.where(inside, query, 0.0).astype(BF16)
+            extra = row_extra(lane, head, (), 1.0)
+            scores = nt_dot(jnp.concatenate([own, extra], axis=1), kx_ref[...])
+            top = jnp.max(scores, axis=1, keepdims=True)
+            probs = jnp.exp(scores - top).astype(BF16)
+            halves.append(nn_dot(probs, vx_ref[...]))
+            tops.append(top)
+        number = jnp.where(lane < 64, halves[0], halves[1])
+        total = pltpu.roll(jnp.where(lane < 64, halves[1], halves[0]), 64, 1)
+        out = number / total
+        o_ref[rows, :] = out.astype(BF16)
+        of_ref[rows, :] = out
+        lse_ref[rows, :] = jnp.where(lane < 64, tops[0], tops[1]) + jnp.log(total)
+        return carry
+
+    lax.fori_loop(0, tokens // block, step, 0)
+
+
+def attend_fwd_kernel(block, length_ref, *refs):
+    attend_fwd_core(block, length_ref[0], *refs)
+
+
+def attend_bwd_kernel(
+    block, length_ref, q_ref, k_ref, v_ref, do_ref, of_ref, lse_ref, dq_ref, dk_ref, dv_ref,
+    kx_ref, vx_ref, kt_ref, dk_acc, dv_acc,
+):
+    tokens = q_ref.shape[0]
+    length = length_ref[0]
+    extra_keys = key_extra(tokens, length)
+    kx_ref[:, :128] = k_ref[...]
+    kx_ref[:, 128:] = extra_keys
+    vx_ref[:, :128] = v_ref[...]
+    vx_ref[:, 128:] = extra_keys
+    turned = k_ref[...].astype(F32).T
+    sub = lax.broadcasted_iota(jnp.int32, (128, tokens), 0)
+    kt_ref[0] = jnp.where(sub < 64, turned, 0.0).astype(BF16)
+    kt_ref[1] = jnp.where(sub < 64, 0.0, turned).astype(BF16)
+    dk_acc[...] = jnp.zeros_like(dk_acc)
+    dv_acc[...] = jnp.zeros_like(dv_acc)
+    same = (
+        lax.broadcasted_iota(jnp.int32, (128, 128), 0) // 64
+        == lax.broadcasted_iota(jnp.int32, (128, 128), 1) // 64
+    ).astype(F32).astype(BF16)
+
+    def step(index, carry):
+        rows = pl.ds(pl.multiple_of(index * block, block), block)
+        lane = lax.broadcasted_iota(jnp.int32, (block, 128), 1)
+        query = q_ref[rows, :].astype(F32) * 0.125
+        grad = do_ref[rows, :].astype(F32)
+        inner = grad * of_ref[rows, :]
+        inner_high = inner.astype(BF16)
+        inner_low = (inner - inner_high.astype(F32)).astype(BF16)
+        delta = nn_dot(inner_high, same) + nn_dot(inner_low, same)
+        lse_terms = split_three(-lse_ref[rows, :])
+        delta_terms = split_three(-delta)
+        dq_t = jnp.zeros((128, block), F32)
+        for head in range(2):
+            inside = (lane < 64) if head == 0 else (lane >= 64)
+            own_q = jnp.where(inside, query, 0.0).astype(BF16)
+            own_g = jnp.where(inside, grad, 0.0).astype(BF16)
+            left_q = jnp.concatenate([own_q, row_extra(lane, head, lse_terms, 1.0)], axis=1)
+            left_g = jnp.concatenate([own_g, row_extra(lane, head, delta_terms, 0.0)], axis=1)
+            probs = jnp.exp(nt_dot(kx_ref[...], left_q))
+            dscore = (probs * nt_dot(vx_ref[...], left_g)).astype(BF16)
+            dv_acc[...] += nn_dot(probs.astype(BF16), own_g)
+            dk_acc[...] += nn_dot(dscore, own_q)
+            dq_t = dq_t + nn_dot(kt_ref[head], dscore)
+        dq_ref[rows, :] = (dq_t.T * 0.125).astype(BF16)
+        return carry
+
+    lax.fori_loop(0, tokens // block, step, 0)
+    dk_ref[...] = dk_acc[...].astype(BF16)
+    dv_ref[...] = dv_acc[...].astype(BF16)
+
+
+BIG = pltpu.CompilerParams(vmem_limit_bytes=56 * 1024 * 1024)
+SMEM_SPEC = pl.BlockSpec(memory_space=pltpu.SMEM)
+
+
+def column_block(tokens, offset):
+    return pl.BlockSpec((tokens, 128), lambda pair: (0, pair + offset))
+
+
+def attend_fwd(q_array, q_at, kv_array, k_at, v_at, length):
+    tokens = q_array.shape[0]
+    features = HEADS * 64
+    out_block = column_block(tokens, 0)
+    return pl.pallas_call(
+        functools.partial(attend_fwd_kernel, 256),
+        grid=(HEADS // 2,),
+        in_specs=[SMEM_SPEC, column_block(tokens, q_at), column_block(tokens, k_at), column_block(tokens, v_at)],
+        out_specs=[out_block] * 3,
+        out_shape=[jax.ShapeDtypeStruct((tokens, features), t) for t in (BF16, F32, F32)],
+        scratch_shapes=[pltpu.VMEM((tokens, 256), BF16), pltpu.VMEM((tokens, 128), BF16), pltpu.VMEM((tokens, 128), BF16)],
+        compiler_params=BIG,
+        name="attend_fwd",
+    )(length, q_array, kv_array, kv_array)
+
+
+def attend_bwd(q_array, q_at, kv_array, k_at, v_at, grad, out_f32, lse, length):
+    tokens = q_array.shape[0]
+    features = HEADS * 64
+    own = column_block(tokens, 0)
+    return pl.pallas_call(
+        functools.partial(attend_bwd_kernel, 256),
+        grid=(HEADS // 2,),
+        in_specs=[SMEM_SPEC, column_block(tokens, q_at), column_block(tokens, k_at), column_block(tokens, v_at), own, own, own],
+        out_specs=[own] * 3,
+        out_shape=[jax.ShapeDtypeStruct((tokens, features), BF16)] * 3,
+        scratch_shapes=[
+            pltpu.VMEM((tokens, 256), BF16),
+            pltpu.VMEM((tokens, 256), BF16),
+            pltpu.VMEM((2, 128, tokens), BF16),
+            pltpu.VMEM((tokens, 128), F32),
+            pltpu.VMEM((tokens, 128), F32),
+        ],
+        compiler_params=BIG,
+        name="attend_bwd",
+    )(length, q_array, kv_array, kv_array, grad, out_f32, lse)
+
+
+def row_stats(residual):
+    mean = jnp.mean(residual, axis=1, keepdims=True)
+    centered = residual - mean
+    inv = lax.rsqrt(jnp.mean(centered * centered, axis=1, keepdims=True) + 1e-05)
+    return centered * inv, inv
+
+
+def norm_back(above, unit, inv, gain):
+    scaled = above * gain
+    return inv * (
+        scaled
+        - jnp.mean(scaled, axis=1, keepdims=True)
+        - unit * jnp.mean(scaled * unit, axis=1, keepdims=True)
+    )
+
+
+def col_sum(value):
+    return jnp.sum(value, axis=0, keepdims=True)
+
+
+def vec(vec_ref, index):
+    return vec_ref[pl.ds(index, 1), :]
+
+
+LANG_ROW = 13
+
+
+def project_kernel(x_ref, enc_ref, win_ref, wkv_ref, vec_ref, low_ref, merged_ref, pair_ref):
+    features = x_ref.shape[1]
+    low = (x_ref[...].astype(F32) + vec(vec_ref, LANG_ROW)).astype(BF16)
+    low_ref[...] = low
+    for part, bias in ((0, 0), (1, None), (2, 1)):
+        cols = pl.ds(part * features, features)
+        out = nn_dot(low, win_ref[:, cols])
+        merged_ref[:, cols] = (out if bias is None else out + vec(vec_ref, bias)).astype(BF16)
+    for part, bias in ((0, None), (1, 4)):
+        cols = pl.ds(part * features, features)
+        out = nn_dot(enc_ref[...], wkv_ref[:, cols])
+        pair_ref[:, cols] = (out if bias is None else out + vec(vec_ref, bias)).astype(BF16)
+
+
+def middle_kernel(x_ref, mixed_ref, wout_ref, wcq_ref, vec_ref, unit_ref, inv_ref, one_ref, cq_ref):
+    branch = nn_dot(mixed_ref[...], wout_ref[...]) + vec(vec_ref, 2)
+    unit, inv = row_stats(x_ref[...].astype(F32) + vec(vec_ref, LANG_ROW) + branch)
+    unit_ref[...] = unit
+    inv_ref[...] = jnp.broadcast_to(inv, inv_ref.shape)
+    one = (unit * vec(vec_ref, 7) + vec(vec_ref, 10)).astype(BF16)
+    one_ref[...] = one
+    cq_ref[...] = (nn_dot(one, wcq_ref[...]) + vec(vec_ref, 3)).astype(BF16)
+
+
+def ffn_kernel(
+    length_ref, cmixed_ref, unit_ref, cot_ref, wco_ref, win_ref, wout_ref, vec_ref, fbias_ref,
+    out_ref, act_ref, low3_ref, two_ref, ghid_ref, res2_ref, low2_ref, gcm_ref, sums_ref, fsum_ref,
+):
+    step = pl.program_id(0)
+    rows = cmixed_ref.shape[0]
+
+    @pl.when(step == 0)
+    def _():
+        sums_ref[...] = jnp.zeros_like(sums_ref)
+        fsum_ref[...] = jnp.zeros_like(fsum_ref)
+
+    normed_one = unit_ref[...] * vec(vec_ref, 7) + vec(vec_ref, 10)
+    branch = nn_dot(cmixed_ref[...], wco_ref[...]) + vec(vec_ref, 5)
+    unit2, inv2 = row_stats(normed_one + branch)
+    gain2 = vec(vec_ref, 8)
+    normed_two = unit2 * gain2 + vec(vec_ref, 11)
+    two = normed_two.astype(BF16)
+    two_ref[...] = two
+    hidden = nn_dot(two, win_ref[...]) + fbias_ref[...]
+    square = hidden * hidden
+    tanh = jnp.tanh(0.7978845608028654 * (hidden + 0.044715 * square * hidden))
+    half = 0.5 * (1.0 + tanh)
+    act = (hidden * half).astype(BF16)
+    act_ref[...] = act
+    slope = half + (0.5 * 0.7978845608028654) * hidden * (1.0 - tanh * tanh) * (1.0 + 3 * 0.044715 * square)
+    unit3, inv3 = row_stats(normed_two + nn_dot(act, wout_ref[...]) + vec(vec_ref, 6))
+    gain3 = vec(vec_ref, 9)
+    live = (lax.broadcasted_iota(jnp.int32, (rows, 1), 0) + step * rows < length_ref[0]).astype(F32)
+    out_ref[...] = ((unit3 * gain3 + vec(vec_ref, 12)) * live).astype(BF16)
+    above3 = cot_ref[...].astype(F32) * live
+    res3 = norm_back(above3, unit3, inv3, gain3)
+    low3 = res3.astype(BF16)
+    low3_ref[...] = low3
+    ghid = (nt_dot(low3, wout_ref[...]) * slope).astype(BF16)
+    ghid_ref[...] = ghid
+    above2 = res3 + nt_dot(ghid, win_ref[...])
+    res2 = norm_back(above2, unit2, inv2, gain2)
+    res2_ref[...] = res2
+    low2 = res2.astype(BF16)
+    low2_ref[...] = low2
+    gcm_ref[...] = nt_dot(low2, wco_ref[...]).astype(BF16)
+    for index, value in (
+        (6, low3.astype(F32)), (5, low2.astype(F32)), (9, above3 * unit3), (12, above3), (8, above2 * unit2), (11, above2),
+    ):
+        sums_ref[index : index + 1, :] += col_sum(value)
+    fsum_ref[...] += col_sum(ghid.astype(F32))
+
+
+def lower_kernel(
+    dq_ref, dck_ref, dcv_ref, res2_ref, unit_ref, inv_ref, wcq_ref, wkv_ref, wout_ref, vec_ref,
+    genc_ref, res1_ref, low1_ref, gmix_ref, sums_ref,
+):
+    features = res2_ref.shape[1]
+
+    @pl.when(pl.program_id(0) == 0)
+    def _():
+        sums_ref[...] = jnp.zeros_like(sums_ref)
+
+    genc_ref[...] = nt_dot(dck_ref[...], wkv_ref[:, :features]) + nt_dot(dcv_ref[...], wkv_ref[:, features:])
+    above = res2_ref[...] + nt_dot(dq_ref[...], wcq_ref[...])
+    unit = unit_ref[...]
+    res1 = norm_back(above, unit, inv_ref[:, :1], vec(vec_ref, 7))
+    res1_ref[...] = res1
+    low1 = res1.astype(BF16)
+    low1_ref[...] = low1
+    gmix_ref[...] = nt_dot(low1, wout_ref[...]).astype(BF16)
+    for index, value in (
+        (2, low1.astype(F32)), (3, dq_ref[...].astype(F32)), (4, dcv_ref[...].astype(F32)), (7, above * unit), (10, above),
+    ):
+        sums_ref[index : index + 1, :] += col_sum(value)
+
+
+def input_kernel(dq_ref, dk_ref, dv_ref, res1_ref, win_ref, gin_ref, sums_ref):
+    features = res1_ref.shape[1]
+
+    @pl.when(pl.program_id(0) == 0)
+    def _():
+        sums_ref[...] = jnp.zeros_like(sums_ref)
+
+    total = res1_ref[...]
+    for part, ref in enumerate((dq_ref, dk_ref, dv_ref)):
+        total = total + nt_dot(ref[...], win_ref[:, part * features : (part + 1) * features])
+    gin_ref[...] = total
+    for index, value in ((0, dq_ref[...].astype(F32)), (1, dv_ref[...].astype(F32)), (LANG_ROW, total)):
+        sums_ref[index : index + 1, :] += col_sum(value)
+
+
+def rows_call(kernel, name, tokens, arrays, outs, block=256):
+    in_specs, operands = [], []
+    for array, kind in arrays:
+        operands.append(array)
+        if kind == "smem":
+            in_specs.append(SMEM_SPEC)
+        elif kind == "row":
+            in_specs.append(pl.BlockSpec((block, array.shape[1]), lambda i: (i, 0)))
+        else:
+            in_specs.append(pl.BlockSpec(array.shape, lambda i: (0, 0)))
+    out_specs, out_shape = [], []
+    for out in outs:
+        if len(out) == 2:
+            out_specs.append(pl.BlockSpec((block, out[0]), lambda i: (i, 0)))
+            out_shape.append(jax.ShapeDtypeStruct((tokens, out[0]), out[1]))
+        else:
+            out_specs.append(pl.BlockSpec(out[:2], lambda i: (0, 0)))
+            out_shape.append(jax.ShapeDtypeStruct(out[:2], out[2]))
+    return pl.pallas_call(
+        kernel,
+        grid=(tokens // block,),
+        in_specs=in_specs,
+        out_specs=out_specs,
+        out_shape=out_shape,
+        compiler_params=BIG,
+        name=name,
+    )(*operands)
+
+
+MESH = pl.DeviceIdType.MESH
+ANY_SPEC = pl.BlockSpec(memory_space=pl.ANY)
+
+
+class Place:
+    def __init__(self, depth):
+        dp, fsdp = lax.axis_index("dp"), lax.axis_index("fsdp")
+        self.depth = depth
+        self.z, self.x = dp // 2, lax.rem(dp, 2)
+        self.y, self.c = fsdp // 2, lax.rem(fsdp, 2)
+        self.fsdp = fsdp
+
+    def dev(self, z=None, x=None, y=None, c=None):
+        z, x = (self.z if z is None else z), (self.x if x is None else x)
+        y, c = (self.y if y is None else y), (self.c if c is None else c)
+        return (2 * z + x, 2 * y + c)
+
+    def ahead(self, d):
+        return lax.rem(self.z + d, self.depth)
+
+    def behind(self, d):
+        return lax.rem(self.z + self.depth - d, self.depth)
+
+    def greet(self):
+        others = [self.dev(z=self.ahead(d)) for d in range(1, self.depth)]
+        others += [self.dev(x=1 - self.x), self.dev(y=1 - self.y), self.dev(c=1 - self.c)]
+        others += [self.dev(y=1 - self.y, c=1 - self.c)]
+        barrier = pltpu.get_barrier_semaphore()
+        for other in others:
+            pl.semaphore_signal(barrier, inc=1, device_id=other, device_id_type=MESH)
+        pl.semaphore_wait(barrier, len(others))
+
+
+def remote(src, dst, send, recv, device):
+    return pltpu.make_async_remote_copy(
+        src_ref=src, dst_ref=dst, send_sem=send, recv_sem=recv, device_id=device, device_id_type=MESH
+    )
+
+
+class Gather:
+    def __init__(self, place, src, dst, local, send, recv, cols=None, flip=False):
+        self.place, self.src, self.dst, self.flip = place, src, dst, flip
+        self.local, self.send, self.recv = local, send, recv
+        self.cols = cols
+        self.sent = []
+
+    def at(self, z, x, y, c):
+        where = (z, x, y, c)
+        return self.dst.at[where] if self.cols is None else self.dst.at[(*where, slice(None), self.cols)]
+
+    def push(self, block, index, device):
+        copy = remote(block, block, self.send.at[index], self.recv.at[index], device)
+        copy.start()
+        self.sent.append(copy)
+
+    def heard(self, block, index):
+        remote(block, block, self.send.at[index], self.recv.at[index], self.place.dev()).wait_recv()
+
+    def along_z(self):
+        p = self.place
+        own = self.at(p.z, p.x, p.y, p.c)
+        src = self.src if self.cols is None else self.src.at[:, self.cols]
+        self.copy = pltpu.make_async_copy(src, own, self.local)
+        self.copy.start()
+        for d in range(1, p.depth):
+            copy = remote(src, own, self.send.at[d - 1], self.recv.at[d - 1], p.dev(z=p.ahead(d)))
+            copy.start()
+            self.sent.append(copy)
+
+    def across_one(self):
+        p = self.place
+        self.copy.wait()
+        for d in range(1, p.depth):
+            self.heard(self.at(p.behind(d), p.x, p.y, p.c), d - 1)
+        other = p.dev(x=1 - p.x) if self.flip else p.dev(y=1 - p.y)
+        self.push(self.at(slice(None), p.x, p.y, p.c), p.depth - 1, other)
+
+    def plane(self, mine, c):
+        p = self.place
+        if self.flip:
+            return self.at(slice(None), slice(None), p.y if mine else 1 - p.y, c)
+        return self.at(slice(None), p.x if mine else 1 - p.x, slice(None), c)
+
+    def across_two(self):
+        p = self.place
+        missing = (1 - p.x, p.y) if self.flip else (p.x, 1 - p.y)
+        self.heard(self.at(slice(None), *missing, p.c), p.depth - 1)
+        block = self.plane(True, p.c)
+        self.push(block, p.depth, p.dev(y=1 - p.y) if self.flip else p.dev(x=1 - p.x))
+        self.push(block, p.depth + 1, p.dev(c=1 - p.c))
+
+    def to_core(self):
+        p = self.place
+        block = self.plane(False, p.c)
+        self.heard(block, p.depth)
+        self.push(block, p.depth + 2, p.dev(c=1 - p.c))
+
+    def whole(self):
+        p = self.place
+        self.heard(self.plane(True, 1 - p.c), p.depth + 1)
+        self.heard(self.plane(False, 1 - p.c), p.depth + 2)
+
+    def finish(self):
+        for copy in self.sent:
+            copy.wait_send()
+
+
+class Exchange:
+    def __init__(self, place, src, dst, local, send, recv):
+        self.place, self.src, self.dst = place, src, dst
+        self.local, self.send, self.recv = local, send, recv
+        self.rows = src.shape[1]
+
+    def block(self, owner):
+        return self.dst.at[pl.ds(pl.multiple_of(owner * self.rows, self.rows), self.rows)]
+
+    def start(self):
+        me = self.place.fsdp
+        self.copy = pltpu.make_async_copy(self.src.at[me], self.block(me), self.local)
+        self.copy.start()
+        self.sent = []
+        for d in range(1, 4):
+            to = lax.rem(me + d, 4)
+            copy = remote(
+                self.src.at[to], self.block(me), self.send.at[d - 1], self.recv.at[d - 1],
+                (lax.axis_index("dp"), to),
+            )
+            copy.start()
+            self.sent.append(copy)
+
+    def whole(self):
+        self.copy.wait()
+        for d in range(1, 4):
+            block = self.block(lax.rem(self.place.fsdp + 4 - d, 4))
+            remote(block, block, self.send.at[d - 1], self.recv.at[d - 1], self.place.dev()).wait_recv()
+
+    def finish(self):
+        for copy in self.sent:
+            copy.wait_send()
+
+
+def flat_cols(ref, cols):
+    value = ref[:, :, :, :, :, cols]
+    return value.reshape(-1, value.shape[-1])
+
+
+def first_kernel(
+    depth, langs,
+    dlen_ref, tag_ref, dec_in, enc_in, cot_in, small_in, in_in, out_in, cq_in, ckv_in, co_in, fin_in, fout_in,
+    w_in, w_out, w_cq, w_ckv, w_co, w_fin, w_fout, x_out, enc_out, cot_out, vec_out, fb_out,
+    low_out, merged_out, pair_out, mixed_out, mixf_out, lse_out,
+    small, win, wkv, x, enc, vecs, fb, low, merged, pair, mixed, mixf, lse, small_cols, kx, va, vb,
+    wlocal, wsend, wrecv, elocal, esend, erecv, osem,
+):
+    p = Place(depth)
+    features = x.shape[1]
+    tokens = x.shape[0]
+    p.greet()
+    jobs = []
+
+    def gather(src, dst, cols=None, flip=False):
+        n = len(jobs)
+        jobs.append(Gather(p, src, dst, wlocal.at[n], wsend.at[n], wrecv.at[n], cols, flip))
+        return jobs[-1]
+
+    def part(i):
+        return pl.ds(i * features, features)
+
+    def half(i):
+        return pl.ds(i * (features // 2), features // 2)
+
+    dec = Exchange(p, dec_in, x, elocal.at[0], esend.at[0], erecv.at[0])
+    encode = Exchange(p, enc_in, enc, elocal.at[1], esend.at[1], erecv.at[1])
+    cot = Exchange(p, cot_in, cot_out, elocal.at[2], esend.at[2], erecv.at[2])
+    g_small = gather(small_in, small)
+    g_k, g_v, g_q = gather(in_in, win, part(1)), gather(in_in, win, part(2), True), gather(in_in, win, part(0))
+    g_ck, g_cv = gather(ckv_in, wkv, part(0)), gather(ckv_in, wkv, part(1))
+    g_out, g_cq, g_co = gather(out_in, w_out), gather(cq_in, w_cq), gather(co_in, w_co)
+    g_fi = [gather(fin_in, w_fin, part(i)) for i in range(4)]
+    g_fo = [gather(fout_in, w_fout, half(i)) for i in range(2)]
+    first = [g_small, g_k, g_v, g_q]
+    second = [g_ck, g_cv]
+    third = [g_out, g_cq, g_co]
+    waves = [first, second, third, g_fi[:2], g_fi[2:], g_fo]
+
+    def move(step, *which):
+        for wave in which:
+            for job in waves[wave]:
+                getattr(job, step)()
+
+    writes = []
+
+    def write(src, dst):
+        copy = pltpu.make_async_copy(src, dst, osem.at[len(writes)])
+        copy.start()
+        writes.append(copy)
+
+    dec.start()
+    move("along_z", 0)
+    move("along_z", 1)
+    move("across_one", 0)
+    move("across_two", 0)
+    encode.start()
+    move("across_one", 1)
+    move("along_z", 2)
+    move("to_core", 0)
+    g_small.whole()
+    for r in range(depth * 8):
+        where = (r // 8, (r // 4) % 2, (r // 2) % 2, r % 2)
+        tile = small[where].astype(F32)
+        small_cols[16 * r : 16 * r + 16, :] = tile[:16]
+        lanes = slice(128 * (r // 2), 128 * (r // 2) + 128)
+        if r % 2 == 0:
+            fb[:, lanes] = tile[16:17]
+        else:
+            fb[:, lanes] += tile[16:17]
+    turned = small_cols[...].T
+    vecs[...] = turned[:16]
+    chosen = lax.broadcasted_iota(jnp.int32, (128, 1), 0) == tag_ref[p.fsdp] + 13
+    lang_row = col_sum(jnp.where(chosen, turned, 0.0))
+    vecs[LANG_ROW : LANG_ROW + 1, :] = lang_row
+    write(vecs, vec_out)
+    write(fb, fb_out)
+    dec.whole()
+    write(x, x_out)
+    low[...] = (x[...].astype(F32) + lang_row).astype(BF16)
+    write(low, low_out)
+
+    def project(source, weight, cols, bias, dest):
+        whole = flat_cols(weight, cols)
+
+        def tile(i, carry):
+            rows = pl.ds(pl.multiple_of(i * 256, 256), 256)
+            out = nn_dot(source[rows, :], whole)
+            dest[rows, cols] = (out if bias is None else out + bias).astype(BF16)
+            return carry
+
+        lax.fori_loop(0, tokens // 256, tile, 0)
+
+    g_k.whole()
+    project(low, win, part(1), None, merged)
+    g_v.whole()
+    project(low, win, part(2), vecs[1:2, :], merged)
+    move("across_two", 1)
+    move("across_one", 2)
+    move("along_z", 3)
+    g_q.whole()
+    project(low, win, part(0), vecs[0:1, :], merged)
+    write(win, w_in)
+    write(merged, merged_out)
+    move("to_core", 1)
+    move("across_two", 2)
+    move("across_one", 3)
+    move("along_z", 4)
+    cot.start()
+    encode.whole()
+    write(enc, enc_out)
+    g_ck.whole()
+    project(enc, wkv, part(0), None, pair)
+    g_cv.whole()
+    project(enc, wkv, part(1), vecs[4:5, :], pair)
+    write(wkv, w_ckv)
+    write(pair, pair_out)
+    steps = [
+        [("to_core", 2), ("across_two", 3), ("across_one", 4), ("along_z", 5)],
+        [("to_core", 3), ("across_two", 4), ("across_one", 5)],
+        [("to_core", 4), ("across_two", 5)],
+        [("to_core", 5)],
+    ]
+    length = dlen_ref[p.fsdp]
+    for pair_index in range(4):
+        cols = pl.ds(128 * pair_index, 128)
+        attend_fwd_core(
+            256, length, merged.at[:, cols], merged.at[:, pl.ds(features + 128 * pair_index, 128)],
+            merged.at[:, pl.ds(2 * features + 128 * pair_index, 128)],
+            mixed.at[:, cols], mixf.at[:, cols], lse.at[:, cols], kx, va, vb,
+        )
+        for step, wave in steps[pair_index]:
+            move(step, wave)
+    write(mixed, mixed_out)
+    write(mixf, mixf_out)
+    write(lse, lse_out)
+    move("whole", 2, 3, 4, 5)
+    cot.whole()
+    for job in (*jobs, dec, encode, cot):
+        job.finish()
+    for copy in writes:
+        copy.wait()
+
+
+def first_call(depth, langs, dlen, tags, dec, enc, cot, small, *weights):
+    groups, part_rows, features = dec.shape
+    tokens = groups * part_rows
+    hidden = weights[5].shape[1]
+
+    def full(w):
+        return (depth, 2, 2, 2, *w.shape)
+
+    def sds(shape, dtype):
+        return jax.ShapeDtypeStruct(shape, dtype)
+
+    outs = [sds(full(w), BF16) for w in weights]
+    outs += [sds((tokens, features), BF16)] * 3 + [sds((16, features), F32), sds((1, hidden), F32)]
+    outs += [sds((tokens, n * features), BF16) for n in (1, 3, 2, 1)] + [sds((tokens, features), F32)] * 2
+    n_jobs = 15
+    return pl.pallas_call(
+        functools.partial(first_kernel, depth, langs),
+        in_specs=[SMEM_SPEC] * 2 + [ANY_SPEC] * 11,
+        out_specs=[ANY_SPEC] * len(outs),
+        out_shape=outs,
+        scratch_shapes=[
+            pltpu.VMEM(full(small), BF16),
+            pltpu.VMEM(full(weights[0]), BF16),
+            pltpu.VMEM(full(weights[3]), BF16),
+            pltpu.VMEM((tokens, features), BF16),
+            pltpu.VMEM((tokens, features), BF16),
+            pltpu.VMEM((16, features), F32),
+            pltpu.VMEM((1, hidden), F32),
+            pltpu.VMEM((tokens, features), BF16),
+            pltpu.VMEM((tokens, 3 * features), BF16),
+            pltpu.VMEM((tokens, 2 * features), BF16),
+            pltpu.VMEM((tokens, features), BF16),
+            pltpu.VMEM((tokens, features), F32),
+            pltpu.VMEM((tokens, features), F32),
+            pltpu.VMEM((features, 128), F32),
+            pltpu.VMEM((tokens, 256), BF16),
+            pltpu.VMEM((tokens, 128), BF16),
+            pltpu.VMEM((tokens, 128), BF16),
+            pltpu.SemaphoreType.DMA((n_jobs,)),
+            pltpu.SemaphoreType.DMA((n_jobs, depth + 3)),
+            pltpu.SemaphoreType.DMA((n_jobs, depth + 3)),
+            pltpu.SemaphoreType.DMA((3,)),
+            pltpu.SemaphoreType.DMA((3, 3)),
+            pltpu.SemaphoreType.DMA((3, 3)),
+            pltpu.SemaphoreType.DMA((16,)),
+        ],
+        compiler_params=pltpu.CompilerParams(
+            vmem_limit_bytes=56 * 1024 * 1024, collective_id=1, has_side_effects=True
+        ),
+        name="first",
+    )(dlen, tags, dec, enc, cot, small, *weights)
+
+
+def fast_body(
+    dec_input, enc_output, dec_lengths, enc_lengths, lang_tags, lang_table, self_in, self_out, cross_q, cross_kv,
+    cross_out, ffn_in, ffn_out, biases, ffn_bias, norm_gains, norm_shifts, cotangent,
+):
+    both = ("dp", "fsdp")
+    groups, part_rows, features = dec_input.shape
+    tokens = groups * part_rows
+    hidden = ffn_in.shape[1]
+    langs = lang_table.shape[1]
+    me = lax.axis_index("fsdp")
+    depth = lax.axis_size("dp") // 2
+    dec_len = lax.dynamic_slice(dec_lengths, (me,), (1,))
+    enc_len = lax.dynamic_slice(enc_lengths, (me,), (1,))
+    tag = lax.dynamic_slice(lang_tags, (me,), (1,))
+    fcols = ffn_bias.shape[0]
+    small = jnp.concatenate([biases, norm_gains, norm_shifts, lang_table], axis=1)
+    small = jnp.pad(small, ((0, 16), (0, 128 - small.shape[1])))
+    small = lax.dynamic_update_slice(small, ffn_bias[None], (16, lax.rem(me, 2) * fcols))
+    (
+        w_in, w_out, w_cq, w_ckv, w_co, w_fin, w_fout, x, enc, cot, vecs, fbias,
+        low, merged, pair, mixed, mixed_f32, self_lse,
+    ) = first_call(
+        depth, langs, dec_lengths, lang_tags, dec_input, enc_output, cotangent.astype(BF16), small,
+        self_in, self_out, cross_q, cross_kv, cross_out, ffn_in, ffn_out,
+    )
+    w_in, w_out, w_cq, w_ckv, w_co, w_fin, w_fout = [
+        w.reshape(-1, w.shape[-1]) for w in (w_in, w_out, w_cq, w_ckv, w_co, w_fin, w_fout)
+    ]
+    onehot = (tag == jnp.arange(langs)).astype(F32)
+    fcols = ffn_bias.shape[0] // biases.shape[0]
+    unit1, inv1, one, cquery = rows_call(
+        middle_kernel, "middle", tokens,
+        [(x, "row"), (mixed, "row"), (w_out, "all"), (w_cq, "all"), (vecs, "all")],
+        [(features, F32), (128, F32), (features, BF16), (features, BF16)],
+    )
+    cmixed, cmixed_f32, cross_lse = attend_fwd(cquery, 0, pair, 0, 4, enc_len)
+    output, act, low3, two, ghid, res2, low2, gcm, sums_a, fsum = rows_call(
+        ffn_kernel, "ffn", tokens,
+        [(dec_len, "smem"), (cmixed, "row"), (unit1, "row"), (cot, "row"), (w_co, "all"), (w_fin, "all"), (w_fout, "all"), (vecs, "all"), (fbias, "all")],
+        [(features, BF16), (hidden, BF16), (features, BF16), (features, BF16), (hidden, BF16), (features, F32), (features, BF16), (features, BF16), (16, features, F32), (1, hidden, F32)],
+    )
+    dcq, dck, dcv = attend_bwd(cquery, 0, pair, 0, 4, gcm, cmixed_f32, cross_lse, enc_len)
+    genc, res1, low1, gmix, sums_b = rows_call(
+        lower_kernel, "lower", tokens,
+        [(dcq, "row"), (dck, "row"), (dcv, "row"), (res2, "row"), (unit1, "row"), (inv1, "row"), (w_cq, "all"), (w_ckv, "all"), (w_out, "all"), (vecs, "all")],
+        [(features, F32), (features, F32), (features, BF16), (features, BF16), (16, features, F32)],
+    )
+    dq, dk, dv = attend_bwd(merged, 0, merged, 4, 8, gmix, mixed_f32, self_lse, dec_len)
+    gin, sums_c = rows_call(
+        input_kernel, "input", tokens,
+        [(dq, "row"), (dk, "row"), (dv, "row"), (res1, "row"), (w_in, "all")],
+        [(features, F32), (16, features, F32)],
+    )
+    g_fout = outer_sum(act, low3)
+    g_fin = outer_sum(two, ghid)
+    g_co = outer_sum(cmixed, low2)
+    g_ckv = jnp.concatenate([outer_sum(enc, dck), outer_sum(enc, dcv)], axis=1)
+    g_cq = outer_sum(one, dcq)
+    g_out = outer_sum(mixed, low1)
+    g_in = jnp.concatenate([outer_sum(low, dq), outer_sum(low, dk), outer_sum(low, dv)], axis=1)
+    sums = sums_a + sums_b + sums_c
+    g_table = sums[LANG_ROW][:, None] * onehot[None, :]
+    g_small = jnp.concatenate([sums[:13].T, g_table, fsum.reshape(features, fcols)], axis=1)
+    g_small = jnp.pad(g_small, ((0, 0), (0, 128 - g_small.shape[1])))
+    parts = lax.axis_size(both) if hasattr(lax, "axis_size") else lax.psum(1, both)
+    packed = jnp.concatenate([g.reshape(parts, -1) for g in (g_fout, g_fin, g_co, g_ckv, g_cq, g_out, g_in, g_small)], axis=1)
+    packed = lax.psum_scatter(packed, both, scatter_dimension=0, tiled=True)[0]
+    shards, at = [], 0
+    for like in (ffn_out, ffn_in, cross_out, cross_kv, cross_q, self_out, self_in, jnp.zeros((biases.shape[0], 128))):
+        shards.append(packed[at : at + like.size].reshape(like.shape))
+        at += like.size
+    r_fout, r_fin, r_co, r_ckv, r_cq, r_out, r_in, r_small = shards
+    output = lax.all_to_all(output[None], "fsdp", 1, 0, tiled=True)
+    gin = lax.all_to_all(gin[None], "fsdp", 1, 0, tiled=True)
+    genc = lax.all_to_all(genc[None], "fsdp", 1, 0, tiled=True)
+    return (
+        output, gin, genc, r_small[:, 13 : 13 + langs], r_in, r_out, r_cq, r_ckv, r_co, r_fin, r_fout,
+        r_small[:, :7], r_small[:, 13 + langs : 13 + langs + fcols].reshape(-1), r_small[:, 7:10], r_small[:, 10:13],
+    )
+
+
 def solution(mesh):
+    def either(*args):
+        whole_sequences = mesh.shape["fsdp"] == args[0].shape[0] and args[3 + 3].shape[0] % 16 == 0
+        return (fast_body if whole_sequences else body)(*args)
+
     return jax.shard_map(
-        body,
+        either,
         mesh=mesh,
         in_specs=(
             P("dp", "fsdp", None),

time: 2330 us -> 629 us (0.27)
  waiting for transfers between devices: 1440 us -> 254 us
  blocking collectives: 366 us -> 0 us
  matrix products: 281 us -> 27.6 us
  Pallas kernels: 0 us -> 212 us
  other arithmetic: 99.8 us -> 16.3 us
  local copies, waits for them, and re-layouts: 117 us -> 84 us
    reduce_scatter x11 -> x0, waiting for transfers between devices: 940 us -> none  [the longest x1 140 us: body(): lax.psum_scatter(grad_ffn_out, ('dp', 'fsdp'), scatter_dimension=0, tiled...]
    unnamed x27 -> x2, waiting for transfers between devices: 478 us -> 167 us
    all_gather x7 -> x0, blocking collectives: 287 us -> none  [the longest x1 43.6 us: body(): lax.all_gather(biases, ('dp', 'fsdp'), axis=0, tiled=True)]
    dot_general x28 -> x0, matrix products: 247 us -> none  [the longest x2 53.3 us: attend_back(): jnp.einsum('sqhd,skhd->shqk', grad_heads, value_heads, preferred_element_...]
    pallas_call x0 -> x8, Pallas kernels: none -> 212 us  [the longest x1 85.3 us: first_call(): pl.pallas_call(functools.partial(first_kernel, depth, langs), in_specs=[S...]
    all_to_all x0 -> x3, waiting for transfers between devices: none -> 86.9 us  [the longest x1 37.6 us: fast_body(): gin = lax.all_to_all(gin[None], 'fsdp', 1, 0, tiled=True)]
    unnamed x2 -> x0, blocking collectives: 78.6 us -> none
    convert_element_type x6 -> x2, other arithmetic: 57.2 us -> 3.34 us  [the longest x1 2.69 us: fast_body(): cotangent.astype(BF16)]
  transfers between devices with their start and end apart: 23 -> 4, of which waited for: 15 -> 4; matrix products, arithmetic and copies ran while one was open for 15% -> 4% of each run, Pallas kernels for 0% -> 0%
where the time goes in v1:
time: 629 us; the launch traced here: 621 us
  waiting for transfers between devices  254 us (40%)
  Pallas kernels  212 us (34%)
  local copies, waits for them, and re-layouts  84 us (13%)
  matrix products  27.6 us (4%)
  other arithmetic  16.3 us (3%)
  between operations  14.9 us (2%)
  starting transfers between devices  11.9 us (2%)
    unnamed x2, waiting for transfers between devices  167 us
    pallas_call x1, Pallas kernels, first_call(): pl.pallas_call(functools.partial(first_kernel, depth, langs), in_specs=[S...  85.3 us
    pallas_call x2, Pallas kernels, attend_bwd(): pl.pallas_call(functools.partial(attend_bwd_kernel, 256), grid=(HEADS //...  60.2 us
    pallas_call x4, Pallas kernels, rows_call(): pl.pallas_call(kernel, grid=(tokens // block,), in_specs=in_specs, out_sp...  43.5 us
    all_to_all x1, waiting for transfers between devices, fast_body(): gin = lax.all_to_all(gin[None], 'fsdp', 1, 0, tiled=True)  37.6 us
    all_to_all x1, waiting for transfers between devices, fast_body(): genc = lax.all_to_all(genc[None], 'fsdp', 1, 0, tiled=True)  32.7 us
    unnamed x66, local copies, waits for them, and re-layouts  29.7 us
    dot_general x10, matrix products, outer_sum(): lax.dot_general(left, right, (((0,), (0,)), ((), ())), preferred_element_...  27.6 us
  transfers between devices with their start and end apart: 4, of which 4 were waited for; matrix products, arithmetic and copies ran while one was open for 4% of the time, Pallas kernels for 0%

profile of v1, /device:TPU:0, one launch (start us, length us, event | category | flops | bytes accessed | tf_op | source)
XLA Modules:
  0.0 620.7 jit_solution(18419607292778333307)
XLA Ops:
  18.1 85.3 %first.1 = (bf16[4,2,2,2,16,1536]{5,4,3,2,1,0:T(8,128)(2,1)}, bf16[4,2,2,2,16,512]{5,4,3,2,1,0:T(8,128)(2,1)}, bf16[4,2,2,2,16,512]{5,4,3,2,1,0:T(8,128)(2,1)}, ...) custom-call(s32[4]{0:T(128)} %dlen_ref.1, ...), custom_call_target="tpu_custom_call" | custom-call | tf_op jit(solution)/shard_map/first/pallas_call | solution.py:1029
  103.4 5.7 middle.1
  109.1 22.8 %attend_fwd.1 = (bf16[1024,512]{1,0:T(8,128)(2,1)}, f32[1024,512]{1,0:T(8,128)}, f32[1024,512]{1,0:T(8,128)}) custom-call(s32[1]{0:T(128)} %dynamic_slice.10.length_ref, bf16[1024,512]{1,0:T(8,128)(2,1)} %get-tuple-element.68.refs_0_.q_ref, bf16[1024,1024]{1,0:T(8,128)(2,1)} %get-tuple-element.69.refs_1_.refs_2_.k_ref.v_ref, ...), custom_call_target="tpu_custom_call" | custom-call | tf_op jit(solution)/shard_map/attend_fwd/pallas_call | solution.py:522
  131.9 22.7 %ffn.1 = (bf16[1024,512]{1,0:T(8,128)(2,1)}, bf16[1024,2048]{1,0:T(8,128)(2,1)}, bf16[1024,512]{1,0:T(8,128)(2,1)}, bf16[1024,512]{1,0:T(8,128)(2,1)}, bf16[1024...) custom-call(s32[1]{0:T(128)} %dynamic_slice.9.length_ref, ...), custom_call_target="tpu_custom_call" | custom-call | tf_op jit(solution)/shard_map/ffn/pallas_call | solution.py:713
  154.7 30.0 %attend_bwd.2 = (bf16[1024,512]{1,0:T(8,128)(2,1)}, bf16[1024,512]{1,0:T(8,128)(2,1)}, bf16[1024,512]{1,0:T(8,128)(2,1)}) custom-call(s32[1]{0:T(128)} %dynamic_slice.10.length_ref, bf16[1024,512]{1,0:T(8,128)(2,1)} %get-tuple-element.68.refs_0_.q_ref, bf16[1024,1024]{1,0:T(8,128)(2,1)} %get-tuple-element.69.refs_1_.refs_2_.k_ref.v_ref, ...), custom_call_target="tpu_custom_call" | custom-call | tf_op jit(solution)/shard_map/attend_bwd/pallas_call | solution.py:538
  188.6 8.6 %lower.1 = (f32[1024,512]{1,0:T(8,128)}, f32[1024,512]{1,0:T(8,128)}, bf16[1024,512]{1,0:T(8,128)(2,1)}, bf16[1024,512]{1,0:T(8,128)(2,1)}, f32[16,512]{1,0:T(8,128)}) custom-call(bf16[1024,512]{1,0:T(8,128)(2,1)} %get-tuple-element.82.dq_ref, bf16[1024,512]{1,0:T(8,128)(2,1)} %get-tuple-element.83.dck_ref, bf16[1024,512]{1,0:T(8,128)(2,1)} %get-tuple-element.84.dcv_ref, ...), custom_call_target="tpu_custom_call" | custom-call | tf_op jit(solution)/shard_map/lower/pallas_call | solution.py:713
  197.2 30.2 %attend_bwd.3 = (bf16[1024,512]{1,0:T(8,128)(2,1)}, bf16[1024,512]{1,0:T(8,128)(2,1)}, bf16[1024,512]{1,0:T(8,128)(2,1)}) custom-call(s32[1]{0:T(128)} %dynamic_slice.9.length_ref, bf16[1024,1536]{1,0:T(8,128)(2,1)} %get-tuple-element.78.q_ref.k_ref.v_ref, bf16[1024,1536]{1,0:T(8,128)(2,1)} %get-tuple-element.78.q_ref.k_ref.v_ref, ...), custom_call_target="tpu_custom_call" | custom-call | tf_op jit(solution)/shard_map/attend_bwd/pallas_call | solution.py:538
  227.4 3.1 fusion.22
  234.1 6.5 %input.1 = (f32[1024,512]{1,0:T(8,128)}, f32[16,512]{1,0:T(8,128)}) custom-call(bf16[1024,512]{1,0:T(8,128)(2,1)} %get-tuple-element.91.dq_ref, bf16[1024,512]{1,0:T(8,128)(2,1)} %get-tuple-element.92.dk_ref, bf16[1024,512]{1,0:T(8,128)(2,1)} %get-tuple-element.93.dv_ref, f32[1024,512]{1,0:T(8,128)} %get-tuple-element.94.res1_ref, bf16[512,1536]{1,0:T(8,128)(2,1)} %bitcast.56), custom_call_target="tpu_custom_call" | custom-call | tf_op jit(solution)/shard_map/input/pallas_call | solution.py:713
  265.5 6.8 %fusion.13 = f32[2048,512]{1,0:T(8,128)} fusion(bf16[1024,2048]{1,0:T(8,128)(2,1)} %get-tuple-element.98, bf16[1024,512]{1,0:T(8,128)(2,1)} %get-tuple-element.99), kind=kOutput, calls=%fused_computation.38 | convolution fusion | flops 2147483648 | bytes 9437184 | tf_op jit(solution)/shard_map/dot_general | solution.py:29
  272.3 5.0 reshape.143
  277.3 6.9 %fusion.14 = f32[512,2048]{1,0:T(8,128)} fusion(bf16[1024,512]{1,0:T(8,128)(2,1)} %get-tuple-element.100, bf16[1024,2048]{1,0:T(8,128)(2,1)} %get-tuple-element.101), kind=kOutput, calls=%fused_computation.39 | convolution fusion | flops 2147483648 | bytes 9437184 | tf_op jit(solution)/shard_map/dot_general | solution.py:29
  284.1 5.1 reshape.144
  289.3 4.6 constant_dynamic-update-slice_fusion.7
  306.8 7.1 %reduce.32 = bf16[1024,512]{1,0:T(8,128)(2,1)S(1)} reduce(bf16[1024,1,512]{2,1,0:T(2,128)(2,1)S(1)} %bitcast.45, bf16[]{:T(256)} %broadcast.53), dimensions={1}, to_apply=%bitcast.42.reduce_sub_computation | reduce | bytes 2097154
  315.9 3.8 all-to-all-start
  319.6 3.5 copy.65
  323.1 16.6 %all-to-all-done = bf16[4,2,65536]{2,1,0:T(2,128)(2,1)S(1)} async-done(((bf16[4,2,65536]{2,1,0:T(2,128)(2,1)}), bf16[4,2,65536]{2,1,0:T(2,128)(2,1)S(1)}, u32[]{:S(2)}, u32[]{:S(2)}) %all-to-all-start) | async-done | bytes 1048608 | tf_op jit(solution)/shard_map/all_to_all | solution.py:1139
  339.8 3.6 all-to-all-start.1
  343.4 5.2 copy.66
  348.6 37.6 %all-to-all-done.1 = f32[1,1024,512]{2,0,1:T(1,128)S(1)} async-done(((f32[1,1024,512]{2,0,1:T(1,128)}), f32[1,1024,512]{2,0,1:T(1,128)S(1)}, u32[]{:S(2)}, u32[]{:S(2)}) %all-to-all-start.1) | async-done | bytes 2097184 | tf_op jit(solution)/shard_map/all_to_all | solution.py:1140
  386.2 4.5 all-to-all-start.2
  395.1 32.7 %all-to-all-done.2 = f32[1,1024,512]{2,0,1:T(1,128)} async-done(((f32[1,1024,512]{2,0,1:T(1,128)}), f32[1,1024,512]{2,0,1:T(1,128)}, u32[]{:S(2)}, u32[]{:S(2)}) %all-to-all-start.2) | async-done | bytes 2097184 | tf_op jit(solution)/shard_map/all_to_all | solution.py:1141
  430.9 167.2 %all-reduce.5.cloned.1.call-done = f32[32,133120]{1,0:T(8,128)} async-done(((f32[32,133120]{1,0:T(8,128)}), f32[32,133120]{1,0:T(8,128)}) %all-reduce.5.cloned.1.call-update) | async-done | bytes 17039376
  (119 shorter events, 80.9 us)
Async XLA Ops:
  7.2 590.9 %all-reduce.5.cloned.1.call-start = ((), (), s32[]{:S(2)}) async-start(), calls=%async_computation.3 | async-start | bytes 34078720
  154.7 30.0 %copy-start.22 = (bf16[1024,512]{1,0:T(8,128)(2,1)S(1)}, bf16[1024,512]{1,0:T(8,128)(2,1)}, u32[]{:S(2)}) copy-start(bf16[1024,512]{1,0:T(8,128)(2,1)} %get-tuple-element.103) | copy-start | bytes 3145732
  184.7 2.1 copy-start.11
  197.2 30.2 %copy-start.20 = (bf16[1024,512]{1,0:T(8,128)(2,1)S(1)}, bf16[1024,512]{1,0:T(8,128)(2,1)}, u32[]{:S(2)}) copy-start(bf16[1024,512]{1,0:T(8,128)(2,1)} %get-tuple-element.106) | copy-start | bytes 3145732
  227.4 3.2 copy-start.13
  227.4 4.9 copy-start.12
  234.0 6.5 %copy-start.16 = (f32[16,512]{1,0:T(8,128)S(1)}, f32[16,512]{1,0:T(8,128)}, u32[]{:S(2)}) copy-start(f32[16,512]{1,0:T(8,128)} %get-tuple-element.107) | copy-start | bytes 98308
  234.0 6.5 %copy-start.17 = (f32[16,512]{1,0:T(8,128)S(1)}, f32[16,512]{1,0:T(8,128)}, u32[]{:S(2)}) copy-start(f32[16,512]{1,0:T(8,128)} %get-tuple-element.108) | copy-start | bytes 98308
  234.0 8.0 %copy-start.14 = (bf16[1024,512]{1,0:T(8,128)(2,1)S(1)}, bf16[1024,512]{1,0:T(8,128)(2,1)}, u32[]{:S(2)}) copy-start(bf16[1024,512]{1,0:T(8,128)(2,1)} %get-tuple-element.70.cmixed_ref) | copy-start | bytes 3145732
  234.1 8.0 %copy-start.19 = (bf16[1024,512]{1,0:T(8,128)(2,1)S(1)}, bf16[1024,512]{1,0:T(8,128)(2,1)}, u32[]{:S(2)}) copy-start(bf16[1024,512]{1,0:T(8,128)(2,1)} %get-tuple-element.102) | copy-start | bytes 3145732
  240.5 3.5 copy-start.10
  248.5 4.7 copy-start.9
  250.4 2.8 copy-start.21
  259.7 2.7 copy-start.18
  289.3 4.6 copy-start
  293.8 2.4 copy-start.4
  293.8 3.5 copy-start.1
  296.2 2.5 copy-start.5
  296.2 3.5 copy-start.6
  313.8 5.8 copy-start.7
  315.9 23.9 %all-to-all-start = ((bf16[4,2,65536]{2,1,0:T(2,128)(2,1)}), bf16[4,2,65536]{2,1,0:T(2,128)(2,1)S(1)}, u32[]{:S(2)}, u32[]{:S(2)}) async-start(bf16[4,2,65536]{2,1,0:T(2,128)(2,1)} %reshape.205), calls=%async_computation | async-start | bytes 2097152 | tf_op jit(solution)/shard_map/all_to_all | solution.py:1139
  339.8 46.4 %all-to-all-start.1 = ((f32[1,1024,512]{2,0,1:T(1,128)}), f32[1,1024,512]{2,0,1:T(1,128)S(1)}, u32[]{:S(2)}, u32[]{:S(2)}) async-start(f32[1,1024,512]{2,0,1:T(1,128)} %copy.65), calls=%async_computation.1 | async-start | bytes 4194304 | tf_op jit(solution)/shard_map/all_to_all | solution.py:1140
  386.2 4.5 copy-start.2
  386.2 41.7 %all-to-all-start.2 = ((f32[1,1024,512]{2,0,1:T(1,128)}), f32[1,1024,512]{2,0,1:T(1,128)}, u32[]{:S(2)}, u32[]{:S(2)}) async-start(f32[1,1024,512]{2,0,1:T(1,128)} %copy.66), calls=%async_computation.2 | async-start | bytes 4194304 | tf_op jit(solution)/shard_map/all_to_all | solution.py:1141
  (3 other events, 3.8 us)
Sparse Core Ops, SparseCore 0:
  303.6 294.5 all-reduce.4
